TPU v7x, 32 devices: a whole 2x2x4 slice. The times are simulated.
32 devices in a mesh: tx: 8 (over y, x, core), ty: 4 (over z).
Axes of the slice: x: 2, y: 2, z: 4, core: 2. Of those that a mesh axis runs over, the one named last changes fastest.
Arguments:
- adjoint_in: float32 [5, 3, 64, 64, 128], P(None, None, 'ty', 'tx'), may hold values from -6 to 6
- courant: float32 [2, 3, 64, 64, 128], P(None, None, 'ty', 'tx'), may hold values from -0.45 to 0.45
- vertical_inverse: float32 [5, 128, 128], replicated, as said below
- links: int32 [40, 4], replicated, may hold values from 0 to 95, as said below
Outputs:
- adjoint_out: float32 [5, 3, 64, 64, 128], P(None, None, 'ty', 'tx')
Inputs may be any that keep to these rules, and one draw needn't show every extreme that they name: `links`: the three panel slots hold three faces of a cube that meet at one corner, in an order drawn afresh; call them X, Y, Z. X's east side joins Y's west side (code 0, both ways, tile row to same tile row), X's north side joins Z's south side (code 1, both ways, tile column to same tile column), Y's north side joins Z's east side with rotation: cell x = i of Y's top row is the neighbour of cell y = i of Z's east column (code 2 for Z's east ghosts, two rows a tile with off 0 and 8; code 3 for Y's north ghosts, one row a tile with off 0 or 8); all other panel sides are open. Row order is drawn afresh. Offsets are 0 or 8, codes 0 to 3. `vertical_inverse`: each block has a diagonal in [0.6, 1.0) and independent off-diagonal entries.
All inputs are finite; a program needn't handle non-finite values.
Results may differ from a plain program's by a relative error of at most 0.0003.
Values sent between devices are 32-bit elements; how exact they have to be, the bound alone decides.
A program may use at most 64 MiB of HBM per device.

v0:
```python
import jax
import jax.numpy as jnp
from jax import lax
from jax.sharding import PartitionSpec as P

STEPS = 2


def with_halo(block, sides, width):
    for axis, dim in sides:
        count = lax.axis_size(axis)
        forward = [(i, i + 1) for i in range(count - 1)]
        forward.append((count - 1, 0))
        backward = [(target, source) for source, target in forward]
        low = lax.ppermute(
            lax.slice_in_dim(block, block.shape[dim] - width, None, axis=dim), axis, forward
        )
        high = lax.ppermute(lax.slice_in_dim(block, 0, width, axis=dim), axis, backward)
        block = jnp.concatenate([low, block, high], axis=dim)
    return block


def broadcast(block, axis, source):
    block = jnp.where(lax.axis_index(axis) == source, block, jnp.zeros_like(block))
    return lax.psum(block, axis)


def link_tables(links, own_tile, tile_count, slot_count):
    source_slot = links[:, 0] // tile_count
    target_slot = links[:, 1] // tile_count
    target_tile = links[:, 1] % tile_count
    offset = links[:, 2]
    link_kind = links[:, 3]
    slot_ids = jnp.arange(slot_count, dtype=jnp.int32)
    target_hot = (target_slot[:, None] == slot_ids[None, :]).astype(jnp.float32)
    source_hot = (source_slot[:, None] == slot_ids[None, :]).astype(jnp.float32)

    def slot_table(wanted):
        chosen = (
            (target_tile == own_tile) & (link_kind == wanted) & ((link_kind != 2) | (offset == 0))
        )
        weight = chosen.astype(jnp.float32)
        return jnp.sum(
            weight[:, None, None] * target_hot[:, :, None] * source_hot[:, None, :], axis=0
        )

    north_source = jnp.max(jnp.where(link_kind == 2, source_slot, 0))
    east_source = jnp.max(jnp.where(link_kind == 3, source_slot, 0))
    return (slot_table(0), slot_table(1), slot_table(2), slot_table(3), north_source, east_source)


def mix_slots(slot_table, pieces):
    return jnp.sum(slot_table[None, :, :, None, None] * pieces[:, None], axis=2)


def on_device(adjoint_in, courant, vertical_inverse, links):
    col_count = lax.axis_size("tx")
    row_count = lax.axis_size("ty")
    column = lax.axis_index("tx")
    row_index = lax.axis_index("ty")
    slot_count = adjoint_in.shape[1]
    cells_y = adjoint_in.shape[2]
    cells_x = adjoint_in.shape[3]
    tile_count = col_count * row_count
    own_tile = row_index * col_count + column
    x_table, y_table, east_table, north_table, north_source, east_source = link_tables(
        links, own_tile, tile_count, slot_count
    )
    at_east = column == col_count - 1
    at_west = column == 0
    at_north = row_index == row_count - 1
    at_south = row_index == 0
    adjoint = adjoint_in
    for step_index in range(STEPS):
        mixed = jnp.einsum(
            "slm,skyxl->skyxm", vertical_inverse, adjoint, precision=lax.Precision.HIGHEST
        )
        fluxes = courant[:, None] * mixed[None]
        padded = with_halo(fluxes, (("tx", 4), ("ty", 3)), 1)
        halo_east = padded[0, :, :, 1:-1, cells_x + 1]
        halo_west = padded[0, :, :, 1:-1, 0]
        halo_north = padded[1, :, :, cells_y + 1, 1:-1]
        halo_south = padded[1, :, :, 0, 1:-1]
        top_rows = lax.dynamic_slice_in_dim(fluxes[1, :, :, cells_y - 1], north_source, 1, 1)
        east_cols = lax.dynamic_slice_in_dim(fluxes[0, :, :, :, cells_x - 1], east_source, 1, 1)
        north_below = broadcast(top_rows, "ty", row_count - 1)
        north_whole = lax.all_gather(north_below, "tx", axis=2, tiled=True)
        east_beside = broadcast(east_cols, "tx", col_count - 1)
        east_whole = lax.all_gather(east_beside, "ty", axis=2, tiled=True)
        north_piece = lax.dynamic_slice_in_dim(north_whole, row_index * cells_y, cells_y, 2)
        east_piece = lax.dynamic_slice_in_dim(east_whole, column * cells_x, cells_x, 2)
        rotated_east = -jnp.sum(east_table, axis=1)[None, :, None, None] * north_piece
        rotated_north = -jnp.sum(north_table, axis=1)[None, :, None, None] * east_piece
        ghost_east = jnp.where(at_east, mix_slots(x_table, halo_east) + rotated_east, halo_east)
        ghost_west = jnp.where(at_west, mix_slots(x_table, halo_west), halo_west)
        ghost_north = jnp.where(
            at_north, mix_slots(y_table, halo_north) + rotated_north, halo_north
        )
        ghost_south = jnp.where(at_south, mix_slots(y_table, halo_south), halo_south)
        x_line = jnp.concatenate(
            [ghost_west[:, :, :, None], fluxes[0], ghost_east[:, :, :, None]], axis=3
        )
        y_line = jnp.concatenate(
            [ghost_south[:, :, None], fluxes[1], ghost_north[:, :, None]], axis=2
        )
        adjoint = (
            mixed
            + 0.5 * (x_line[:, :, :, 2:] - x_line[:, :, :, :-2])
            + 0.5 * (y_line[:, :, 2:] - y_line[:, :, :-2])
        )
    return adjoint


def solution(mesh):
    placed = (P(None, None, "ty", "tx", None), P(None, None, "ty", "tx", None), P(), P())
    return jax.shard_map(
        on_device,
        mesh=mesh,
        in_specs=placed,
        out_specs=P(None, None, "ty", "tx", None),
        check_vma=False,
    )
```

profile of v0, /device:TPU:0, one launch (start us, length us, event | category | flops | bytes accessed | tf_op | source)
XLA Modules:
  0.0 178.6 jit_solution(6658720027340490278)
XLA Ops:
  0.0 1.2 copy.186
  1.2 0.2 copy-done
  1.3 1.9 %fusion.13 = f32[5,3,16,8,128]{4,3,2,1,0:T(8,128)S(1)} fusion(f32[5,3,16,8,128]{4,3,2,1,0:T(8,128)S(1)} %copy-done, f32[5,128,128]{2,1,0:T(8,128)} %param.6), kind=kOutput, calls=%fused_computation.33 | convolution fusion | flops 377487360 | bytes 2293760 | tf_op jit(solution)/shard_map/slm,skyxl->skyxm/dot_general | solution.py:75
  3.3 0.9 copy-done.1
  4.2 0.2 copy.187
  4.4 0.2 broadcast_multiply_fusion.1
  4.6 0.8 fusion.36
  5.4 0.5 collective-permute-start.1
  5.9 2.9 %collective-permute-start = (f32[2,5,3,16,1,128]{5,3,2,1,4,0:T(8,128)}, f32[2,5,3,16,1,128]{5,3,2,1,4,0:T(8,128)}, u32[]{:S(2)}, u32[]{:S(2)}) collective-permute-start(f32[2,5,3,16,1,128]{5,3,2,1,4,0:T(8,128)} %get-tuple-element.33), channel_id=1, source_target_pairs={{4,0},{8,4},{12,8},{16,12},{20,16},{24,20},{28,24},{0,28},{5,1},{9... | collective-permute-start | bytes 737288 | tf_op jit(solution)/shard_map/ppermute | solution.py:18
  8.8 0.7 fusion.28
  12.5 0.6 neg.18
  13.1 0.5 neg.19
  14.3 20.5 %psum.28 = f32[5,1,8,128]{3,2,0,1:T(8,128)} all-reduce(f32[5,1,8,128]{3,2,0,1:T(8,128)S(1)} %bitcast.157), channel_id=1, replica_groups=mesh['tx'=8,'ty'=4] {'ty'}, use_global_device_ids=true, to_apply=%region_4.5 | all-reduce | flops 5120 | bytes 40960 | tf_op jit(solution)/shard_map/psum | solution.py:25
  35.5 22.7 %psum.29 = f32[5,1,16,128]{3,2,0,1:T(8,128)S(1)} all-reduce(f32[5,1,16,128]{3,2,0,1:T(8,128)S(1)} %select_bitcast_fusion.1), channel_id=1, replica_groups=mesh['tx'=8,'ty'=4] {'tx'}, use_global_device_ids=true, to_apply=%region_10.11 | all-reduce | flops 10240 | bytes 81920 | tf_op jit(solution)/shard_map/psum | solution.py:25
  58.3 13.5 %all_gather.13 = f32[5,1,64,128]{3,2,0,1:T(8,128)S(1)} all-gather(f32[5,1,16,128]{3,2,0,1:T(8,128)S(1)} %psum.29), channel_id=1, replica_groups=mesh['tx'=8,'ty'=4] {'ty'}, dimensions={2}, use_global_device_ids=true | all-gather | bytes 204800 | tf_op jit(solution)/shard_map/all_gather | solution.py:89
  71.7 9.5 %all_gather.12 = f32[5,1,64,128]{3,2,0,1:T(8,128)S(1)} all-gather(f32[5,1,8,128]{3,2,0,1:T(8,128)} %psum.28), channel_id=1, replica_groups=mesh['tx'=8,'ty'=4] {'tx'}, dimensions={2}, use_global_device_ids=true | all-gather | bytes 184320 | tf_op jit(solution)/shard_map/all_gather | solution.py:87
  81.2 0.1 slice_bitcast_fusion.2
  81.4 1.3 pad_maximum_fusion.13
  82.7 0.1 collective-permute-start.2
  82.8 1.9 %collective-permute-start.3 = (f32[2,5,3,1,10,128]{5,3,2,1,4,0:T(1,128)S(1)}, f32[2,5,3,1,10,128]{5,3,2,1,4,0:T(1,128)S(1)}, u32[]{:S(2)}, u32[]{:S(2)}) collective-permute-start(f32[2,5,3,1,10,128]{5,3,2,1,4,0:T(1,128)S(1)} %get-tuple-element.25), channel_id=1, source_target_pairs={{0,1},{1,2},{2,3},{3,0},{4,5},{5,6},{6,7},{7,4},{8,9},{9,10},{10,1... | collective-permute-start | bytes 460808 | tf_op jit(solution)/shard_map/ppermute | solution.py:15
  84.8 0.9 slice_bitcast_fusion.4
  85.7 0.9 slice_bitcast_fusion.5
  86.7 1.0 bitcast_select_fusion.2
  87.7 0.9 bitcast_select_fusion.1
  88.8 0.7 collective-permute-done.2
  89.5 2.8 %collective-permute-done.3 = f32[2,5,3,1,10,128]{5,3,2,1,4,0:T(1,128)S(1)} collective-permute-done((f32[2,5,3,1,10,128]{5,3,2,1,4,0:T(1,128)S(1)}, f32[2,5,3,1,10,128]{5,3,2,1,4,0:T(1,128)S(1)}, u32[]{:S(2)}, u32[]{:S(2)}) %collective-permute-start.3) | collective-permute-done | bytes 153632 | tf_op jit(solution)/shard_map/ppermute | solution.py:15
  92.6 0.2 broadcast_select_fusion.4
  92.7 0.3 fusion.5
  93.0 1.7 fusion.9
  94.8 0.2 copy.201
  95.0 0.2 broadcast_multiply_fusion
  95.1 0.6 copy-done.3
  95.8 0.8 fusion.35
  96.6 1.4 slice_bitcast_fusion
  98.1 23.2 %psum.31 = f32[5,1,16,128]{3,2,0,1:T(8,128)S(1)} all-reduce(f32[5,1,16,128]{3,2,0,1:T(8,128)S(1)} %select_bitcast_fusion), channel_id=1, replica_groups=mesh['tx'=8,'ty'=4] {'tx'}, use_global_device_ids=true, to_apply=%region_16.17 | all-reduce | flops 10240 | bytes 81920 | tf_op jit(solution)/shard_map/psum | solution.py:25
  121.3 13.4 %all_gather.15 = f32[5,1,64,128]{3,2,0,1:T(8,128)S(1)} all-gather(f32[5,1,16,128]{3,2,0,1:T(8,128)S(1)} %psum.31), channel_id=1, replica_groups=mesh['tx'=8,'ty'=4] {'ty'}, dimensions={2}, use_global_device_ids=true | all-gather | bytes 204800 | tf_op jit(solution)/shard_map/all_gather | solution.py:89
  134.7 2.6 %collective-permute-start.4 = (f32[2,5,3,16,1,128]{5,3,2,1,4,0:T(8,128)}, f32[2,5,3,16,1,128]{5,3,2,1,4,0:T(8,128)S(1)}, u32[]{:S(2)}, u32[]{:S(2)}) collective-permute-start(f32[2,5,3,16,1,128]{5,3,2,1,4,0:T(8,128)} %get-tuple-element.29), channel_id=1, source_target_pairs={{4,0},{8,4},{12,8},{16,12},{20,16},{24,20},{28,24},{0,28},{5,1},{9... | collective-permute-start | bytes 737288 | tf_op jit(solution)/shard_map/ppermute | solution.py:18
  137.4 2.5 %copy.252 = f32[1,5,3,16,8,128]{5,4,3,2,1,0:T(8,128)} copy(f32[1,5,3,16,8,128]{5,3,2,1,4,0:T(8,128)} %get-tuple-element.27) | data formatting | bytes 1966080 | tf_op jit(solution)/shard_map/slice | solution.py:101
  139.9 17.6 %psum.30 = f32[5,1,8,128]{3,2,0,1:T(8,128)S(1)} all-reduce(f32[5,1,8,128]{3,2,0,1:T(8,128)S(1)} %bitcast.156), channel_id=1, replica_groups=mesh['tx'=8,'ty'=4] {'ty'}, use_global_device_ids=true, to_apply=%region_13.14 | all-reduce | flops 5120 | bytes 40960 | tf_op jit(solution)/shard_map/psum | solution.py:25
  157.5 8.7 %all_gather.14 = f32[5,1,64,128]{3,2,0,1:T(8,128)S(1)} all-gather(f32[5,1,8,128]{3,2,0,1:T(8,128)S(1)} %psum.30), channel_id=1, replica_groups=mesh['tx'=8,'ty'=4] {'tx'}, dimensions={2}, use_global_device_ids=true | all-gather | bytes 184320 | tf_op jit(solution)/shard_map/all_gather | solution.py:87
  166.2 0.2 pad_maximum_fusion.10
  166.5 2.0 %collective-permute-start.7 = (f32[2,5,3,1,10,128]{5,3,2,1,4,0:T(1,128)S(1)}, f32[2,5,3,1,10,128]{5,3,2,1,4,0:T(1,128)S(1)}, u32[]{:S(2)}, u32[]{:S(2)}) collective-permute-start(f32[2,5,3,1,10,128]{5,3,2,1,4,0:T(1,128)S(1)} %get-tuple-element.23), channel_id=1, source_target_pairs={{0,1},{1,2},{2,3},{3,0},{4,5},{5,6},{6,7},{7,4},{8,9},{9,10},{10,1... | collective-permute-start | bytes 460808 | tf_op jit(solution)/shard_map/ppermute | solution.py:15
  168.6 0.1 multiply_reduce_fusion.1
  168.8 4.4 %collective-permute-done.6 = f32[2,5,3,1,10,128]{5,3,2,1,4,0:T(1,128)S(1)} collective-permute-done((f32[2,5,3,1,10,128]{5,3,2,1,4,0:T(1,128)S(1)}, f32[2,5,3,1,10,128]{5,3,2,1,4,0:T(1,128)S(1)}, u32[]{:S(2)}, u32[]{:S(2)}) %collective-permute-start.6) | collective-permute-done | bytes 153632 | tf_op jit(solution)/shard_map/ppermute | solution.py:18
  173.3 2.8 %collective-permute-done.7 = f32[2,5,3,1,10,128]{5,3,2,1,4,0:T(1,128)S(1)} collective-permute-done((f32[2,5,3,1,10,128]{5,3,2,1,4,0:T(1,128)S(1)}, f32[2,5,3,1,10,128]{5,3,2,1,4,0:T(1,128)S(1)}, u32[]{:S(2)}, u32[]{:S(2)}) %collective-permute-start.7) | collective-permute-done | bytes 153632 | tf_op jit(solution)/shard_map/ppermute | solution.py:15
  176.3 0.2 broadcast_select_fusion.3
  176.5 0.3 fusion
  176.8 1.8 fusion.4
  (66 shorter events, 1.4 us)
Async XLA Ops:
  0.0 1.3 copy-start
  3.3 0.9 copy-start.1
  4.4 4.3 %copy-start.8 = (s32[40,4]{0,1:T(4,128)S(1)}, s32[40,4]{0,1:T(4,128)}, u32[]{:S(2)}) copy-start(s32[40,4]{0,1:T(4,128)} %param.7) | copy-start | bytes 1924
  5.4 75.9 %collective-permute-start.1 = (f32[2,5,3,16,1,128]{5,3,2,1,4,0:T(8,128)}, f32[2,5,3,16,1,128]{5,3,2,1,4,0:T(8,128)}, u32[]{:S(2)}, u32[]{:S(2)}) collective-permute-start(f32[2,5,3,16,1,128]{5,3,2,1,4,0:T(8,128)} %get-tuple-element.32), channel_id=1, source_target_pairs={{0,4},{4,8},{8,12},{12,16},{16,20},{20,24},{24,28},{28,0},{1,5},{5... | collective-permute-start | bytes 737288 | tf_op jit(solution)/shard_map/ppermute | solution.py:15
  5.9 75.5 %collective-permute-start = (f32[2,5,3,16,1,128]{5,3,2,1,4,0:T(8,128)}, f32[2,5,3,16,1,128]{5,3,2,1,4,0:T(8,128)}, u32[]{:S(2)}, u32[]{:S(2)}) collective-permute-start(f32[2,5,3,16,1,128]{5,3,2,1,4,0:T(8,128)} %get-tuple-element.33), channel_id=1, source_target_pairs={{4,0},{8,4},{12,8},{16,12},{20,16},{24,20},{28,24},{0,28},{5,1},{9... | collective-permute-start | bytes 737288 | tf_op jit(solution)/shard_map/ppermute | solution.py:18
  81.3 5.4 %copy-start.10 = (f32[3]{0:T(128)S(1)}, f32[3]{0:T(128)}, u32[]{:S(2)}) copy-start(f32[3]{0:T(128)} %neg.18) | copy-start | bytes 40
  82.7 6.8 %collective-permute-start.2 = (f32[2,5,3,1,10,128]{5,3,2,1,4,0:T(1,128)S(1)}, f32[2,5,3,1,10,128]{5,3,2,1,4,0:T(1,128)S(1)}, u32[]{:S(2)}, u32[]{:S(2)}) collective-permute-start(f32[2,5,3,1,10,128]{5,3,2,1,4,0:T(1,128)S(1)} %get-tuple-element.24), channel_id=1, source_target_pairs={{1,0},{2,1},{3,2},{0,3},{5,4},{6,5},{7,6},{4,7},{9,8},{10,9},{11,1... | collective-permute-start | bytes 460808 | tf_op jit(solution)/shard_map/ppermute | solution.py:18
  82.8 9.5 %collective-permute-start.3 = (f32[2,5,3,1,10,128]{5,3,2,1,4,0:T(1,128)S(1)}, f32[2,5,3,1,10,128]{5,3,2,1,4,0:T(1,128)S(1)}, u32[]{:S(2)}, u32[]{:S(2)}) collective-permute-start(f32[2,5,3,1,10,128]{5,3,2,1,4,0:T(1,128)S(1)} %get-tuple-element.25), channel_id=1, source_target_pairs={{0,1},{1,2},{2,3},{3,0},{4,5},{5,6},{6,7},{7,4},{8,9},{9,10},{10,1... | collective-permute-start | bytes 460808 | tf_op jit(solution)/shard_map/ppermute | solution.py:15
  86.7 5.9 %copy-start.9 = (f32[3]{0:T(128)S(1)}, f32[3]{0:T(128)}, u32[]{:S(2)}) copy-start(f32[3]{0:T(128)} %neg.19) | copy-start | bytes 40
  88.7 4.3 %copy-start.2 = (f32[5,3,16,8,128]{4,3,2,1,0:T(8,128)S(1)}, f32[5,3,16,8,128]{4,3,2,1,0:T(8,128)}, u32[]{:S(2)}) copy-start(f32[5,3,16,8,128]{4,3,2,1,0:T(8,128)} %copy-done.1) | copy-start | bytes 2949124
  88.8 4.3 %copy-start.7 = (f32[5,128,128]{2,1,0:T(8,128)S(1)}, f32[5,128,128]{2,1,0:T(8,128)}, u32[]{:S(2)}) copy-start(f32[5,128,128]{2,1,0:T(8,128)} %param.6) | copy-start | bytes 983044
  94.8 0.9 copy-start.3
  134.7 31.5 %collective-permute-start.5 = (f32[2,5,3,16,1,128]{5,3,2,1,4,0:T(8,128)}, f32[2,5,3,16,1,128]{5,3,2,1,4,0:T(8,128)S(1)}, u32[]{:S(2)}, u32[]{:S(2)}) collective-permute-start(f32[2,5,3,16,1,128]{5,3,2,1,4,0:T(8,128)} %get-tuple-element.28), channel_id=1, source_target_pairs={{0,4},{4,8},{8,12},{12,16},{16,20},{20,24},{24,28},{28,0},{1,5},{5... | collective-permute-start | bytes 737288 | tf_op jit(solution)/shard_map/ppermute | solution.py:15
  134.7 31.5 %collective-permute-start.4 = (f32[2,5,3,16,1,128]{5,3,2,1,4,0:T(8,128)}, f32[2,5,3,16,1,128]{5,3,2,1,4,0:T(8,128)S(1)}, u32[]{:S(2)}, u32[]{:S(2)}) collective-permute-start(f32[2,5,3,16,1,128]{5,3,2,1,4,0:T(8,128)} %get-tuple-element.29), channel_id=1, source_target_pairs={{4,0},{8,4},{12,8},{16,12},{20,16},{24,20},{28,24},{0,28},{5,1},{9... | collective-permute-start | bytes 737288 | tf_op jit(solution)/shard_map/ppermute | solution.py:18
  166.4 10.1 %copy-start.5 = (f32[5,3,16,8,128]{4,2,1,0,3:T(8,128)S(1)}, f32[5,3,16,8,128]{4,2,1,0,3:T(8,128)}, u32[]{:S(2)}) copy-start(f32[5,3,16,8,128]{4,2,1,0,3:T(8,128)} %get-tuple-element.26) | copy-start | bytes 2949124
  166.4 6.8 %collective-permute-start.6 = (f32[2,5,3,1,10,128]{5,3,2,1,4,0:T(1,128)S(1)}, f32[2,5,3,1,10,128]{5,3,2,1,4,0:T(1,128)S(1)}, u32[]{:S(2)}, u32[]{:S(2)}) collective-permute-start(f32[2,5,3,1,10,128]{5,3,2,1,4,0:T(1,128)S(1)} %get-tuple-element.22), channel_id=1, source_target_pairs={{1,0},{2,1},{3,2},{0,3},{5,4},{6,5},{7,6},{4,7},{9,8},{10,9},{11,1... | collective-permute-start | bytes 460808 | tf_op jit(solution)/shard_map/ppermute | solution.py:18
  166.5 9.6 %collective-permute-start.7 = (f32[2,5,3,1,10,128]{5,3,2,1,4,0:T(1,128)S(1)}, f32[2,5,3,1,10,128]{5,3,2,1,4,0:T(1,128)S(1)}, u32[]{:S(2)}, u32[]{:S(2)}) collective-permute-start(f32[2,5,3,1,10,128]{5,3,2,1,4,0:T(1,128)S(1)} %get-tuple-element.23), channel_id=1, source_target_pairs={{0,1},{1,2},{2,3},{3,0},{4,5},{5,6},{6,7},{7,4},{8,9},{9,10},{10,1... | collective-permute-start | bytes 460808 | tf_op jit(solution)/shard_map/ppermute | solution.py:15
  168.8 8.0 %copy-start.4 = (f32[5,3,16,8,128]{4,3,2,1,0:T(8,128)S(1)}, f32[5,3,16,8,128]{4,3,2,1,0:T(8,128)}, u32[]{:S(2)}) copy-start(f32[5,3,16,8,128]{4,3,2,1,0:T(8,128)} %copy-done.3) | copy-start | bytes 2949124
  168.8 8.0 %copy-start.6 = (f32[1,5,3,16,8,128]{5,4,3,2,1,0:T(8,128)S(1)}, f32[1,5,3,16,8,128]{5,4,3,2,1,0:T(8,128)}, u32[]{:S(2)}) copy-start(f32[1,5,3,16,8,128]{5,4,3,2,1,0:T(8,128)} %copy.252) | copy-start | bytes 2949124
where the time goes:
time: 179 us
  blocking collectives  129 us (72%)
  local copies, waits for them, and re-layouts  11.1 us (6%)
  waiting for transfers between devices  10.7 us (6%)
  starting transfers between devices  10.1 us (6%)
  other arithmetic  9.29 us (5%)
  between operations  4.59 us (3%)
  matrix products  3.63 us (2%)
    psum x4, blocking collectives, broadcast(): return lax.psum(block, axis)  84 us
    all_gather x2, blocking collectives, on_device(): east_whole = lax.all_gather(east_beside, 'ty', axis=2, tiled=True)  26.9 us
    all_gather x2, blocking collectives, on_device(): north_whole = lax.all_gather(north_below, 'tx', axis=2, tiled=True)  18.2 us
    ppermute x4, starting transfers between devices, with_halo(): lax.ppermute(lax.slice_in_dim(block, 0, width, axis=dim), axis, backward)  5.73 us
    ppermute x4, waiting for transfers between devices, with_halo(): lax.ppermute(lax.slice_in_dim(block, block.shape[dim] - width, None, axis...  5.56 us
    ppermute x4, waiting for transfers between devices, with_halo(): lax.ppermute(lax.slice_in_dim(block, 0, width, axis=dim), axis, backward)  5.12 us
    ppermute x4, starting transfers between devices, with_halo(): lax.ppermute(lax.slice_in_dim(block, block.shape[dim] - width, None, axis...  4.4 us
    dot_general x2, matrix products, on_device(): jnp.einsum('slm,skyxl->skyxm', vertical_inverse, adjoint, precision=lax.P...  3.63 us
  transfers between devices with their start and end apart: 8, of which 4 were waited for; matrix products, arithmetic and copies ran while one was open for 5% of the time, Pallas kernels for 0%

commit v1 on v0

--- a/solution.py
+++ b/solution.py
@@ -22,7 +22,7 @@
 
 def broadcast(block, axis, source):
     block = jnp.where(lax.axis_index(axis) == source, block, jnp.zeros_like(block))
-    return lax.psum(block, axis)
+    return jnp.sum(lax.all_gather(block, axis), axis=0)
 
 
 def link_tables(links, own_tile, tile_count, slot_count):

time: 179 us -> 143 us (0.80)
  blocking collectives: 129 us -> 91.3 us
    psum x4 -> x0, blocking collectives: 84 us -> none  [broadcast(): return lax.psum(block, axis)]
    all_gather x0 -> x4, blocking collectives: none -> 45.2 us  [broadcast(): return jnp.sum(lax.all_gather(block, axis), axis=0)]
    ppermute x4, starting transfers between devices: 5.73 us -> 10.7 us  [with_halo(): lax.ppermute(lax.slice_in_dim(block, 0, width, axis=dim), axis, backward)]
    ppermute x4, starting transfers between devices: 4.4 us -> 1.12 us  [with_halo(): lax.ppermute(lax.slice_in_dim(block, block.shape[dim] - width, None, axis...]
    unnamed x23 -> x27, local copies, waits for them, and re-layouts: 2.87 us -> 3.64 us
  transfers between devices with their start and end apart: 8 -> 8, of which waited for: 4 -> 3; matrix products, arithmetic and copies ran while one was open for 5% -> 6% of each run, Pallas kernels for 0% -> 0%
where the time goes in v1:
time: 143 us; the launch traced here: 142 us
  blocking collectives  91.3 us (64%)
  starting transfers between devices  11.8 us (8%)
  local copies, waits for them, and re-layouts  11.4 us (8%)
  waiting for transfers between devices  10.1 us (7%)
  other arithmetic  9.8 us (7%)
  between operations  4.24 us (3%)
  matrix products  3.63 us (3%)
    all_gather x4, blocking collectives, broadcast(): return jnp.sum(lax.all_gather(block, axis), axis=0)  45.2 us
    all_gather x2, blocking collectives, on_device(): east_whole = lax.all_gather(east_beside, 'ty', axis=2, tiled=True)  27.8 us
    all_gather x2, blocking collectives, on_device(): north_whole = lax.all_gather(north_below, 'tx', axis=2, tiled=True)  18.2 us
    ppermute x4, starting transfers between devices, with_halo(): lax.ppermute(lax.slice_in_dim(block, 0, width, axis=dim), axis, backward)  10.7 us
    ppermute x4, waiting for transfers between devices, with_halo(): lax.ppermute(lax.slice_in_dim(block, block.shape[dim] - width, None, axis...  5.91 us
    ppermute x4, waiting for transfers between devices, with_halo(): lax.ppermute(lax.slice_in_dim(block, 0, width, axis=dim), axis, backward)  4.23 us
    unnamed x27, local copies, waits for them, and re-layouts  3.64 us
    dot_general x2, matrix products, on_device(): jnp.einsum('slm,skyxl->skyxm', vertical_inverse, adjoint, precision=lax.P...  3.63 us
  transfers between devices with their start and end apart: 8, of which 3 were waited for; matrix products, arithmetic and copies ran while one was open for 6% of the time, Pallas kernels for 0%

profile of v1, /device:TPU:0, one launch (start us, length us, event | category | flops | bytes accessed | tf_op | source)
XLA Modules:
  0.0 142.3 jit_solution(10310639860936791499)
XLA Ops:
  0.0 1.2 copy.244
  1.2 0.2 copy-done
  1.3 1.9 %fusion.13 = f32[5,3,16,8,128]{4,3,2,1,0:T(8,128)S(1)} fusion(f32[5,3,16,8,128]{4,3,2,1,0:T(8,128)S(1)} %copy-done, f32[5,128,128]{2,1,0:T(8,128)} %param.6), kind=kOutput, calls=%fused_computation.33 | convolution fusion | flops 377487360 | bytes 2293760 | tf_op jit(solution)/shard_map/slm,skyxl->skyxm/dot_general | solution.py:75
  3.3 0.9 copy-done.1
  4.2 0.2 copy.245
  4.4 0.2 broadcast_multiply_fusion.1
  4.6 0.8 fusion.36
  5.4 0.5 collective-permute-start.1
  5.9 2.9 %collective-permute-start = (f32[2,5,3,16,1,128]{5,3,2,1,4,0:T(8,128)}, f32[2,5,3,16,1,128]{5,3,2,1,4,0:T(8,128)}, u32[]{:S(2)}, u32[]{:S(2)}) collective-permute-start(f32[2,5,3,16,1,128]{5,3,2,1,4,0:T(8,128)} %get-tuple-element.33), channel_id=1, source_target_pairs={{4,0},{8,4},{12,8},{16,12},{20,16},{24,20},{28,24},{0,28},{5,1},{9... | collective-permute-start | bytes 737288 | tf_op jit(solution)/shard_map/ppermute | solution.py:18
  8.8 0.7 fusion.28
  12.0 0.7 slice.161
  13.5 14.2 %all-gather = f32[4,5,1,1,8,128]{5,4,3,2,1,0:T(8,128)S(1)} all-gather(f32[1,5,1,1,8,128]{5,4,3,2,1,0:T(8,128)S(1)} %copy.246), channel_id=2, replica_groups=mesh['tx'=8,'ty'=4] {'ty'}, dimensions={0}, use_global_device_ids=true | all-gather | bytes 102400 | tf_op jit(solution)/shard_map/all_gather | solution.py:25
  27.7 9.4 %all-gather.1 = f32[5,64,128]{2,1,0:T(8,128)S(1)} all-gather(f32[5,8,128]{2,1,0:T(8,128)S(1)} %reduce.6), channel_id=3, replica_groups=mesh['tx'=8,'ty'=4] {'tx'}, dimensions={1}, use_global_device_ids=true | all-gather | bytes 184320 | tf_op jit(solution)/shard_map/all_gather | solution.py:87
  37.8 0.8 select_bitcast_fusion.1
  38.6 8.5 %all-gather.2 = f32[8,5,1,16,1,128]{5,3,4,2,1,0:T(8,128)S(1)} all-gather(f32[1,5,1,16,1,128]{5,3,4,2,1,0:T(8,128)S(1)} %select_bitcast_fusion.1), channel_id=4, replica_groups=mesh['tx'=8,'ty'=4] {'tx'}, dimensions={0}, use_global_device_ids=true | all-gather | bytes 368640 | tf_op jit(solution)/shard_map/all_gather | solution.py:25
  47.2 14.3 %all-gather.3 = f32[5,64,128]{2,1,0:T(8,128)} all-gather(f32[5,16,128]{2,1,0:T(8,128)S(1)} %bitcast_reduce_fusion.1), channel_id=5, replica_groups=mesh['tx'=8,'ty'=4] {'ty'}, dimensions={1}, use_global_device_ids=true | all-gather | bytes 204800 | tf_op jit(solution)/shard_map/all_gather | solution.py:89
  61.5 0.7 constant_dynamic-slice_fusion.2
  62.2 0.1 slice_bitcast_fusion.2
  62.4 1.3 pad_maximum_fusion.13
  63.7 3.8 %collective-permute-start.2 = (f32[2,5,3,1,10,128]{5,3,2,1,4,0:T(1,128)S(1)}, f32[2,5,3,1,10,128]{5,3,2,1,4,0:T(1,128)S(1)}, u32[]{:S(2)}, u32[]{:S(2)}) collective-permute-start(f32[2,5,3,1,10,128]{5,3,2,1,4,0:T(1,128)S(1)} %get-tuple-element.24), channel_id=1, source_target_pairs={{1,0},{2,1},{3,2},{0,3},{5,4},{6,5},{7,6},{4,7},{9,8},{10,9},{11,1... | collective-permute-start | bytes 460808 | tf_op jit(solution)/shard_map/ppermute | solution.py:18
  67.5 0.9 slice_bitcast_fusion.4
  68.4 0.9 slice_bitcast_fusion.5
  69.4 1.0 bitcast_select_fusion.2
  70.4 0.9 bitcast_select_fusion.1
  71.5 2.9 %collective-permute-done.3 = f32[2,5,3,1,10,128]{5,3,2,1,4,0:T(1,128)S(1)} collective-permute-done((f32[2,5,3,1,10,128]{5,3,2,1,4,0:T(1,128)S(1)}, f32[2,5,3,1,10,128]{5,3,2,1,4,0:T(1,128)S(1)}, u32[]{:S(2)}, u32[]{:S(2)}) %collective-permute-start.3) | collective-permute-done | bytes 153632 | tf_op jit(solution)/shard_map/ppermute | solution.py:15
  74.7 0.2 broadcast_select_fusion.4
  74.9 0.3 fusion.5
  75.2 1.7 %fusion.9 = f32[5,3,16,8,128]{4,3,2,1,0:T(8,128)S(1)} fusion(f32[5,3,16,8,128]{4,2,1,0,3:T(8,128)S(1)} %fusion.5, f32[5,3,16,8,128]{4,3,2,1,0:T(8,128)S(1)} %copy-done.2, f32[5,3,16,8,128]{4,2,1,0,3:T(8,128)S(1)} %fusion.7, f32[5,128,128]{2,1,0:T(8,128)S(1)} %copy-done.6), kind=kOutput, calls=%fused_computation.23 | convolution fusion | flops 378224640 | bytes 4259840 | tf_op jit(solution)/shard_map/slm,skyxl->skyxm/dot_general | solution.py:75
  76.9 0.2 copy.263
  77.1 0.2 broadcast_multiply_fusion
  77.3 0.6 copy-done.3
  77.9 0.7 slice.171
  78.6 1.4 %slice_bitcast_fusion = (f32[5,3,16,8,128]{4,2,1,0,3:T(8,128)}, f32[1,5,3,16,8,128]{5,3,2,1,4,0:T(8,128)}) fusion(f32[2,5,3,16,8,128]{5,3,2,1,4,0:T(8,128)S(1)} %broadcast_multiply_fusion), kind=kLoop, calls=%fused_computation.3 | loop fusion | bytes 3932160 | tf_op jit(solution)/shard_map/squeeze | solution.py:104
  80.1 13.2 %all-gather.4 = f32[4,5,1,1,8,128]{5,4,3,2,1,0:T(8,128)S(1)} all-gather(f32[1,5,1,1,8,128]{5,4,3,2,1,0:T(8,128)S(1)} %copy.265), channel_id=6, replica_groups=mesh['tx'=8,'ty'=4] {'ty'}, dimensions={0}, use_global_device_ids=true | all-gather | bytes 102400 | tf_op jit(solution)/shard_map/all_gather | solution.py:25
  93.3 0.8 select_bitcast_fusion
  94.1 9.3 %all-gather.6 = f32[8,5,1,16,1,128]{5,3,4,2,1,0:T(8,128)S(1)} all-gather(f32[1,5,1,16,1,128]{5,3,4,2,1,0:T(8,128)S(1)} %select_bitcast_fusion), channel_id=8, replica_groups=mesh['tx'=8,'ty'=4] {'tx'}, dimensions={0}, use_global_device_ids=true | all-gather | bytes 368640 | tf_op jit(solution)/shard_map/all_gather | solution.py:25
  103.5 13.5 %all-gather.7 = f32[5,64,128]{2,1,0:T(8,128)S(1)} all-gather(f32[5,16,128]{2,1,0:T(8,128)S(1)} %bitcast_reduce_fusion), channel_id=9, replica_groups=mesh['tx'=8,'ty'=4] {'ty'}, dimensions={1}, use_global_device_ids=true | all-gather | bytes 204800 | tf_op jit(solution)/shard_map/all_gather | solution.py:89
  117.0 2.6 %collective-permute-start.4 = (f32[2,5,3,16,1,128]{5,3,2,1,4,0:T(8,128)S(1)}, f32[2,5,3,16,1,128]{5,3,2,1,4,0:T(8,128)S(1)}, u32[]{:S(2)}, u32[]{:S(2)}) collective-permute-start(f32[2,5,3,16,1,128]{5,3,2,1,4,0:T(8,128)S(1)} %get-tuple-element.29), channel_id=1, source_target_pairs={{4,0},{8,4},{12,8},{16,12},{20,16},{24,20},{28,24},{0,28},{5,1},{9... | collective-permute-start | bytes 737288 | tf_op jit(solution)/shard_map/ppermute | solution.py:18
  119.6 1.5 %copy.318 = f32[1,5,3,16,8,128]{5,4,3,2,1,0:T(8,128)S(1)} copy(f32[1,5,3,16,8,128]{5,3,2,1,4,0:T(8,128)} %get-tuple-element.27) | data formatting | bytes 1966080 | tf_op jit(solution)/shard_map/slice | solution.py:101
  121.2 8.8 %all-gather.5 = f32[5,64,128]{2,1,0:T(8,128)S(1)} all-gather(f32[5,8,128]{2,1,0:T(8,128)S(1)} %reduce.8), channel_id=7, replica_groups=mesh['tx'=8,'ty'=4] {'tx'}, dimensions={1}, use_global_device_ids=true | all-gather | bytes 184320 | tf_op jit(solution)/shard_map/all_gather | solution.py:87
  130.0 0.2 pad_maximum_fusion.10
  130.2 1.4 collective-permute-start.6
  131.6 0.7 collective-permute-start.7
  132.6 4.2 %collective-permute-done.6 = f32[2,5,3,1,10,128]{5,3,2,1,4,0:T(1,128)S(1)} collective-permute-done((f32[2,5,3,1,10,128]{5,3,2,1,4,0:T(1,128)S(1)}, f32[2,5,3,1,10,128]{5,3,2,1,4,0:T(1,128)S(1)}, u32[]{:S(2)}, u32[]{:S(2)}) %collective-permute-start.6) | collective-permute-done | bytes 153632 | tf_op jit(solution)/shard_map/ppermute | solution.py:18
  136.9 3.0 %collective-permute-done.7 = f32[2,5,3,1,10,128]{5,3,2,1,4,0:T(1,128)S(1)} collective-permute-done((f32[2,5,3,1,10,128]{5,3,2,1,4,0:T(1,128)S(1)}, f32[2,5,3,1,10,128]{5,3,2,1,4,0:T(1,128)S(1)}, u32[]{:S(2)}, u32[]{:S(2)}) %collective-permute-start.7) | collective-permute-done | bytes 153632 | tf_op jit(solution)/shard_map/ppermute | solution.py:15
  140.1 0.2 broadcast_select_fusion.3
  140.3 0.3 fusion
  140.6 1.8 %fusion.4 = f32[5,3,16,8,128]{4,3,2,1,0:T(8,128)} fusion(f32[5,3,16,8,128]{4,3,2,1,0:T(8,128)S(1)} %copy-done.4, f32[5,3,16,8,128]{4,3,2,1,0:T(8,128)S(1)} %bitcast.129, f32[5,3,16,1,128]{4,3,2,1,0:T(1,128)S(1)} %bitcast.139, f32[5,3,16,1,128]{4,3,2,1,0:T(1,128)S(1)} %bitcast.138, f32[5,3,16,8,128]{4,2,1,0,3:T(8,128)S(1)} %fusion), kind=kLoop, calls=%fused_computation.8 | loop fusion | flops 1720320 | bytes 4177920 | tf_op jit(solution)/shard_map/add | solution.py:107
  (68 shorter events, 1.5 us)
Async XLA Ops:
  0.0 1.3 copy-start
  3.3 0.9 copy-start.1
  4.4 4.3 %copy-start.7 = (s32[40,4]{0,1:T(4,128)S(1)}, s32[40,4]{0,1:T(4,128)}, u32[]{:S(2)}) copy-start(s32[40,4]{0,1:T(4,128)} %param.7) | copy-start | bytes 1924
  5.4 57.0 %collective-permute-start.1 = (f32[2,5,3,16,1,128]{5,3,2,1,4,0:T(8,128)}, f32[2,5,3,16,1,128]{5,3,2,1,4,0:T(8,128)}, u32[]{:S(2)}, u32[]{:S(2)}) collective-permute-start(f32[2,5,3,16,1,128]{5,3,2,1,4,0:T(8,128)} %get-tuple-element.32), channel_id=1, source_target_pairs={{0,4},{4,8},{8,12},{12,16},{16,20},{20,24},{24,28},{28,0},{1,5},{5... | collective-permute-start | bytes 737288 | tf_op jit(solution)/shard_map/ppermute | solution.py:15
  5.9 56.5 %collective-permute-start = (f32[2,5,3,16,1,128]{5,3,2,1,4,0:T(8,128)}, f32[2,5,3,16,1,128]{5,3,2,1,4,0:T(8,128)}, u32[]{:S(2)}, u32[]{:S(2)}) collective-permute-start(f32[2,5,3,16,1,128]{5,3,2,1,4,0:T(8,128)} %get-tuple-element.33), channel_id=1, source_target_pairs={{4,0},{8,4},{12,8},{16,12},{20,16},{24,20},{28,24},{0,28},{5,1},{9... | collective-permute-start | bytes 737288 | tf_op jit(solution)/shard_map/ppermute | solution.py:18
  12.9 56.5 %copy-start.8 = (f32[3]{0:T(128)}, f32[3]{0:T(128)S(1)}, u32[]{:S(2)}) copy-start(f32[3]{0:T(128)S(1)} %neg.18) | copy-start | bytes 40
  63.7 7.8 %collective-permute-start.2 = (f32[2,5,3,1,10,128]{5,3,2,1,4,0:T(1,128)S(1)}, f32[2,5,3,1,10,128]{5,3,2,1,4,0:T(1,128)S(1)}, u32[]{:S(2)}, u32[]{:S(2)}) collective-permute-start(f32[2,5,3,1,10,128]{5,3,2,1,4,0:T(1,128)S(1)} %get-tuple-element.24), channel_id=1, source_target_pairs={{1,0},{2,1},{3,2},{0,3},{5,4},{6,5},{7,6},{4,7},{9,8},{10,9},{11,1... | collective-permute-start | bytes 460808 | tf_op jit(solution)/shard_map/ppermute | solution.py:18
  67.5 7.0 %collective-permute-start.3 = (f32[2,5,3,1,10,128]{5,3,2,1,4,0:T(1,128)S(1)}, f32[2,5,3,1,10,128]{5,3,2,1,4,0:T(1,128)S(1)}, u32[]{:S(2)}, u32[]{:S(2)}) collective-permute-start(f32[2,5,3,1,10,128]{5,3,2,1,4,0:T(1,128)S(1)} %get-tuple-element.25), channel_id=1, source_target_pairs={{0,1},{1,2},{2,3},{3,0},{4,5},{5,6},{6,7},{7,4},{8,9},{9,10},{10,1... | collective-permute-start | bytes 460808 | tf_op jit(solution)/shard_map/ppermute | solution.py:15
  71.4 3.7 %copy-start.2 = (f32[5,3,16,8,128]{4,3,2,1,0:T(8,128)S(1)}, f32[5,3,16,8,128]{4,3,2,1,0:T(8,128)}, u32[]{:S(2)}) copy-start(f32[5,3,16,8,128]{4,3,2,1,0:T(8,128)} %copy-done.1) | copy-start | bytes 2949124
  71.5 3.7 %copy-start.6 = (f32[5,128,128]{2,1,0:T(8,128)S(1)}, f32[5,128,128]{2,1,0:T(8,128)}, u32[]{:S(2)}) copy-start(f32[5,128,128]{2,1,0:T(8,128)} %param.6) | copy-start | bytes 983044
  76.9 0.9 copy-start.3
  117.0 13.0 %collective-permute-start.5 = (f32[2,5,3,16,1,128]{5,3,2,1,4,0:T(8,128)S(1)}, f32[2,5,3,16,1,128]{5,3,2,1,4,0:T(8,128)S(1)}, u32[]{:S(2)}, u32[]{:S(2)}) collective-permute-start(f32[2,5,3,16,1,128]{5,3,2,1,4,0:T(8,128)S(1)} %get-tuple-element.28), channel_id=1, source_target_pairs={{0,4},{4,8},{8,12},{12,16},{16,20},{20,24},{24,28},{28,0},{1,5},{5... | collective-permute-start | bytes 737288 | tf_op jit(solution)/shard_map/ppermute | solution.py:15
  117.0 13.0 %collective-permute-start.4 = (f32[2,5,3,16,1,128]{5,3,2,1,4,0:T(8,128)S(1)}, f32[2,5,3,16,1,128]{5,3,2,1,4,0:T(8,128)S(1)}, u32[]{:S(2)}, u32[]{:S(2)}) collective-permute-start(f32[2,5,3,16,1,128]{5,3,2,1,4,0:T(8,128)S(1)} %get-tuple-element.29), channel_id=1, source_target_pairs={{4,0},{8,4},{12,8},{16,12},{20,16},{24,20},{28,24},{0,28},{5,1},{9... | collective-permute-start | bytes 737288 | tf_op jit(solution)/shard_map/ppermute | solution.py:18
  130.0 2.5 %copy-start.9 = (f32[3]{0:T(128)S(1)}, f32[3]{0:T(128)}, u32[]{:S(2)}) copy-start(f32[3]{0:T(128)} %copy-done.8) | copy-start | bytes 40
  130.2 10.1 %copy-start.5 = (f32[5,3,16,8,128]{4,2,1,0,3:T(8,128)S(1)}, f32[5,3,16,8,128]{4,2,1,0,3:T(8,128)}, u32[]{:S(2)}) copy-start(f32[5,3,16,8,128]{4,2,1,0,3:T(8,128)} %get-tuple-element.26) | copy-start | bytes 2949124
  130.2 6.6 %collective-permute-start.6 = (f32[2,5,3,1,10,128]{5,3,2,1,4,0:T(1,128)S(1)}, f32[2,5,3,1,10,128]{5,3,2,1,4,0:T(1,128)S(1)}, u32[]{:S(2)}, u32[]{:S(2)}) collective-permute-start(f32[2,5,3,1,10,128]{5,3,2,1,4,0:T(1,128)S(1)} %get-tuple-element.22), channel_id=1, source_target_pairs={{1,0},{2,1},{3,2},{0,3},{5,4},{6,5},{7,6},{4,7},{9,8},{10,9},{11,1... | collective-permute-start | bytes 460808 | tf_op jit(solution)/shard_map/ppermute | solution.py:18
  131.6 8.2 %collective-permute-start.7 = (f32[2,5,3,1,10,128]{5,3,2,1,4,0:T(1,128)S(1)}, f32[2,5,3,1,10,128]{5,3,2,1,4,0:T(1,128)S(1)}, u32[]{:S(2)}, u32[]{:S(2)}) collective-permute-start(f32[2,5,3,1,10,128]{5,3,2,1,4,0:T(1,128)S(1)} %get-tuple-element.23), channel_id=1, source_target_pairs={{0,1},{1,2},{2,3},{3,0},{4,5},{5,6},{6,7},{7,4},{8,9},{9,10},{10,1... | collective-permute-start | bytes 460808 | tf_op jit(solution)/shard_map/ppermute | solution.py:15
  132.5 8.0 %copy-start.4 = (f32[5,3,16,8,128]{4,3,2,1,0:T(8,128)S(1)}, f32[5,3,16,8,128]{4,3,2,1,0:T(8,128)}, u32[]{:S(2)}) copy-start(f32[5,3,16,8,128]{4,3,2,1,0:T(8,128)} %copy-done.3) | copy-start | bytes 2949124
